TPU v7x, 32 devices: a whole 2x2x4 slice. The times are simulated.
32 devices in a mesh: groups: 2 (over x), pts: 8 (over z, y), branch: 2 (over core).
Axes of the slice: x: 2, y: 2, z: 4, core: 2. Of those that a mesh axis runs over, the one named last changes fastest.
Arguments:
- point_feat: bfloat16 [2, 65536, 128], P('branch', ('groups', 'pts')), parts along dimension 1, may hold values from -6 to 6
- query_feat: bfloat16 [2, 8192, 768], P('branch', ('groups', 'pts')), parts along dimension 1, may hold values from -640 to 640
- supernode_query: bfloat16 [2, 512, 768], P('branch', ('groups', 'pts')), parts along dimension 1, may hold values from -1000 to 1000
- route_owner: int32 [2, 512, 1], P('branch', 'groups'), parts along dimension 1, may hold values from 0 to 7; in each aligned block of 32 rows (0 to 31, 32 to 63, ..., all dimensions but the last counted through in order) at most 8 rows name the same one
- route_slot: int32 [2, 512], P('branch', 'groups'), parts along dimension 1, may hold values from 0 to 31
- anchor_index: int32 [2, 384], P('branch', 'groups'), parts along dimension 1, may hold values from 0 to 255, as said below
- w_in: bfloat16 [2, 128, 768], P('branch'), may hold values from -0.5 to 0.5
- w_mid: bfloat16 [2, 768, 768], P('branch'), may hold values from -0.21875 to 0.21875
- w_q: bfloat16 [2, 768, 768], P('branch'), may hold values from -0.21875 to 0.21875
- w_kv: bfloat16 [2, 768, 1536], P('branch'), may hold values from -0.21875 to 0.21875
- w_out: bfloat16 [2, 1536, 768], P('branch'), may hold values from -1.25 to 1.25
Outputs:
- result: bfloat16 [2, 8192, 768], P('branch', ('groups', 'pts')), parts along dimension 1
There are 2 independent parts, one for each index of `groups`. A program takes and returns all parts, laid end to end along the dimension named above; an argument that names none is the same for every part. Nothing has to cross between parts.
Inputs may be any that keep to these rules, and one draw needn't show every extreme that they name: `route_owner`: within the rows of one device, at most 8 blocks name one owner, and in every draw some device sends exactly 8 blocks to one owner. `anchor_index`: the 192 entries of each branch are distinct.
All inputs are finite; a program needn't handle non-finite values.
Results may differ from a plain program's by a relative error of at most 0.014.
The roundings to bfloat16 on the way count: a program that leaves them out, or rounds other values in their place, can miss the bound.
Values may be sent and summed in bfloat16 or wider, within the bound.
A program may use at most 128 MiB of HBM per device.

v0:
```python
import math

import jax
import jax.numpy as jnp
from jax import lax
from jax.sharding import PartitionSpec as P

D = 768
HEADS = 12
BLK = 128


def swapped(block, axis, bit):
    count = lax.axis_size(axis)
    route = []
    for low in range(count):
        high = low | 1 << bit
        if high != low and high < count:
            route += [(low, high), (high, low)]
    return lax.ppermute(block, axis, route)


def pool_blocks(blocks, queries, head_size):
    block_count, block_rows, model_width = blocks.shape
    head_count = model_width // head_size
    split_rows = blocks.reshape(block_count, block_rows, head_count, head_size)
    asked_rows = queries.reshape(block_count, head_count, head_size)
    scores = jnp.einsum(
        "nrhe,nhe->nhr", split_rows, asked_rows, preferred_element_type=jnp.float32
    ) / math.sqrt(head_size)
    weights = jax.nn.softmax(scores, axis=-1).astype(jnp.bfloat16)
    pooled = jnp.einsum("nhr,nrhe->nhe", weights, split_rows, preferred_element_type=jnp.float32)
    return pooled.astype(jnp.bfloat16).reshape(block_count, model_width)


def attend(queries, key_rows, value_rows, head_size):
    query_count, model_width = queries.shape
    head_count = model_width // head_size
    query_heads = queries.reshape(query_count, head_count, head_size)
    key_heads = key_rows.reshape(key_rows.shape[0], head_count, head_size)
    value_heads = value_rows.reshape(value_rows.shape[0], head_count, head_size)
    scores = jnp.einsum(
        "qhe,khe->hqk", query_heads, key_heads, preferred_element_type=jnp.float32
    ) / math.sqrt(head_size)
    weights = jax.nn.softmax(scores, axis=-1).astype(jnp.bfloat16)
    output = jnp.einsum("hqk,khe->qhe", weights, value_heads, preferred_element_type=jnp.float32)
    return output.astype(jnp.bfloat16).reshape(query_count, model_width)


def per_device(
    point_feat,
    query_feat,
    supernode_query,
    route_owner,
    route_slot,
    anchor_index,
    w_in,
    w_mid,
    w_q,
    w_kv,
    w_out,
):
    head_size = D // HEADS
    shard_count = lax.axis_size("pts")
    my_index = lax.axis_index("pts")
    points = point_feat[0]
    hidden = jax.nn.gelu(jnp.dot(points, w_in[0], preferred_element_type=jnp.float32)).astype(
        jnp.bfloat16
    )
    encoded = jnp.dot(hidden, w_mid[0], preferred_element_type=jnp.float32).astype(jnp.bfloat16)
    nblocks = points.shape[0] // BLK
    model_width = encoded.shape[1]
    blocks = encoded.reshape(nblocks, BLK, model_width)
    owners = route_owner[0][:, 0].reshape(shard_count, nblocks)
    node_slots = route_slot[0].reshape(shard_count, nblocks)
    block_order = jnp.arange(nblocks, dtype=jnp.int32)
    earlier = block_order[None, :] < block_order[:, None]
    same_owner = owners[:, :, None] == owners[:, None, :]
    block_rank = jnp.sum(same_owner & earlier[None], axis=2)
    my_owner = lax.dynamic_index_in_dim(owners, my_index, 0, keepdims=False)
    my_rank = lax.dynamic_index_in_dim(block_rank, my_index, 0, keepdims=False)
    my_slot = lax.dynamic_index_in_dim(node_slots, my_index, 0, keepdims=False)
    capacity = max(2, 2 * nblocks // shard_count)
    target = my_owner * capacity + my_rank
    place_ids = jnp.arange(capacity, dtype=jnp.int32)
    is_arriving = (owners[:, None, :] == my_index) & (
        block_rank[:, None, :] == place_ids[None, :, None]
    )
    arriving = (jnp.sum(jnp.where(is_arriving, node_slots[:, None, :] + 1, 0), axis=2) - 1).reshape(
        -1
    )
    own_queries = supernode_query[0]
    nodes_here = own_queries.shape[0]
    all_queries = lax.all_gather(own_queries, "pts", axis=0, tiled=True)
    block_queries = jnp.take(all_queries, my_owner * nodes_here + my_slot, axis=0)
    pooled = pool_blocks(blocks, block_queries, head_size)
    outgoing = jnp.zeros((shard_count * capacity, model_width), jnp.bfloat16).at[target].set(pooled)
    received = lax.all_to_all(outgoing, "pts", split_axis=0, concat_axis=0, tiled=True)
    node_ids = jnp.arange(nodes_here, dtype=jnp.int32)
    member = arriving[None, :] == node_ids[:, None]
    pooled_sum = jnp.dot(member.astype(jnp.bfloat16), received, preferred_element_type=jnp.float32)
    node_count = jnp.sum(member.astype(jnp.float32), axis=1)
    combined = own_queries.astype(jnp.float32) + pooled_sum / jnp.maximum(node_count, 1.0)[:, None]
    node_feat = (
        combined * lax.rsqrt(jnp.mean(combined * combined, axis=1, keepdims=True) + 1e-06)
    ).astype(jnp.bfloat16)
    anchor_rows = anchor_index[0]
    all_nodes = lax.all_gather(node_feat, "pts", axis=0, tiled=True)
    anchor_kv = jnp.dot(
        jnp.take(all_nodes, anchor_rows, axis=0), w_kv[0], preferred_element_type=jnp.float32
    ).astype(jnp.bfloat16)
    partner_kv = swapped(anchor_kv, "branch", 0)
    queries = jnp.dot(query_feat[0], w_q[0], preferred_element_type=jnp.float32).astype(
        jnp.bfloat16
    )
    query_count = queries.shape[0]
    query_step = min(512, query_count)

    def answer(query_rows):
        self_out = attend(
            query_rows, anchor_kv[:, :model_width], anchor_kv[:, model_width:], head_size
        )
        cross_out = attend(
            query_rows, partner_kv[:, :model_width], partner_kv[:, model_width:], head_size
        )
        return jnp.concatenate([self_out, cross_out], axis=1)

    joined = lax.map(answer, queries.reshape(query_count // query_step, query_step, model_width))
    joined = joined.reshape(query_count, 2 * model_width)
    result = jnp.dot(joined, w_out[0], preferred_element_type=jnp.float32).astype(jnp.bfloat16)
    return result[None]


def solution(mesh):
    return jax.shard_map(
        per_device,
        mesh=mesh,
        in_specs=(
            P("branch", ("groups", "pts"), None),
            P("branch", ("groups", "pts"), None),
            P("branch", ("groups", "pts"), None),
            P("branch", "groups", None),
            P("branch", "groups"),
            P("branch", "groups"),
            P("branch", None, None),
            P("branch", None, None),
            P("branch", None, None),
            P("branch", None, None),
            P("branch", None, None),
        ),
        out_specs=P("branch", ("groups", "pts"), None),
        check_vma=False,
    )
```

profile of v0, /device:TPU:0, one launch (start us, length us, event | category | flops | bytes accessed | tf_op | source)
XLA Modules:
  0.0 156.5 jit_solution(16071785381284778061)
XLA Ops:
  0.0 0.5 broadcast.172
  0.5 1.5 reduce.7
  2.1 1.3 reduce.6
  3.6 11.2 %convolution_convert_fusion = bf16[4096,768]{1,0:T(8,128)(2,1)} fusion(bf16[1,768,768]{2,1,0:T(8,128)(2,1)} %param.18, bf16[1,4096,128]{2,1,0:T(8,128)(2,1)} %param.11, bf16[1,128,768]{2,1,0:T(8,128)(2,1)} %param.17), kind=kOutput, calls=%fused_computation.16 | convolution fusion | flops 5668601856 | bytes 8716288 | tf_op jit(solution)/shard_map/dot_general | solution.py:70
  14.8 8.8 %copy.24 = bf16[4096,768]{0,1:T(8,128)(2,1)} copy(bf16[4096,768]{1,0:T(8,128)(2,1)} %convolution_convert_fusion) | data formatting | bytes 12582912 | tf_op jit(solution)/shard_map/convert_element_type | solution.py:70
  23.5 7.5 %copy.35 = bf16[96,8,32,128]{3,2,1,0:T(8,128)(2,1)} copy(bf16[96,8,32,128]{3,1,2,0:T(8,128)(2,1)} %bitcast.98) | data formatting | bytes 12582912
  31.0 32.9 %all-gather = bf16[1,256,768]{2,1,0:T(8,128)(2,1)S(1)} all-gather(bf16[1,32,768]{2,1,0:T(8,128)(2,1)S(1)} %copy-done.2), channel_id=2, replica_groups=mesh['groups'=2,'pts'=8,'branch'=2] {'pts'}, dimensions={1}, use_global_device_ids=true | all-gather | bytes 442368 | tf_op jit(solution)/shard_map/all_gather | solution.py:94
  63.9 0.3 convert_reduce_fusion
  64.3 0.6 gather_fusion
  65.2 9.2 %fusion.19 = f32[32,12,1,128]{3,2,1,0:T(1,128)S(1)} fusion(bf16[32,128,12,64]{1,0,3,2:T(8,128)(2,1)} %bitcast.99, bf16[32,12,64,1]{2,1,0,3:T(8,128)(2,1)S(1)} %select_bitcast_fusion), kind=kOutput, calls=%fused_computation.23 | convolution fusion | flops 6291456 | bytes 6537216 | tf_op jit(solution)/shard_map/nrhe,nhe->nhr/dot_general | solution.py:28
  74.4 0.2 fusion.57
  74.6 9.5 %fusion.17 = bf16[32,12,1,64]{3,2,1,0:T(2,128)(2,1)S(1)} fusion(bf16[32,128,12,64]{1,0,3,2:T(8,128)(2,1)} %bitcast.100, bf16[32,12,128,1]{2,0,1,3:T(8,128)(2,1)S(1)} %fusion.57), kind=kOutput, calls=%fused_computation.21 | convolution fusion | flops 6291456 | bytes 6438912 | tf_op jit(solution)/shard_map/nhr,nrhe->nhe/dot_general | solution.py:32
  84.2 1.3 scatter_custom_fusion
  85.5 5.7 %all-to-all-start = ((bf16[8,8,768]{2,1,0:T(8,128)(2,1)}), bf16[8,8,768]{2,1,0:T(8,128)(2,1)S(1)}, u32[]{:S(2)}, u32[]{:S(2)}) async-start(bf16[8,8,768]{2,1,0:T(8,128)(2,1)} %bitcast.15), calls=%async_computation | async-start | bytes 196608 | tf_op jit(solution)/shard_map/all_to_all | solution.py:98
  91.2 0.2 select_reduce_fusion
  91.7 2.3 %convolution_convert_fusion.2 = bf16[512,768]{1,0:T(8,128)(2,1)S(1)} fusion(bf16[1,768,768]{2,1,0:T(8,128)(2,1)} %param.19, bf16[1,512,768]{2,1,0:T(8,128)(2,1)} %param.12), kind=kOutput, calls=%fused_computation.47 | convolution fusion | flops 604372992 | bytes 2752512 | tf_op jit(solution)/shard_map/dot_general | solution.py:113
  94.0 1.2 copy.26
  95.1 3.2 %all-to-all-done = bf16[8,8,768]{2,1,0:T(8,128)(2,1)S(1)} async-done(((bf16[8,8,768]{2,1,0:T(8,128)(2,1)}), bf16[8,8,768]{2,1,0:T(8,128)(2,1)S(1)}, u32[]{:S(2)}, u32[]{:S(2)}) %all-to-all-start) | async-done | bytes 98336 | tf_op jit(solution)/shard_map/all_to_all | solution.py:98
  98.3 0.2 multiply_reduce_fusion.2
  98.6 31.0 %all_gather.7 = bf16[256,768]{1,0:T(8,128)(2,1)S(1)} all-gather(bf16[32,768]{1,0:T(8,128)(2,1)S(1)} %multiply_convert_fusion), channel_id=1, replica_groups=mesh['groups'=2,'pts'=8,'branch'=2] {'pts'}, dimensions={0}, use_global_device_ids=true | all-gather | bytes 442368 | tf_op jit(solution)/shard_map/all_gather | solution.py:108
  129.6 1.0 gather_fusion.1
  130.7 2.3 %convolution_convert_fusion.1 = bf16[192,1536]{1,0:T(8,128)(2,1)S(1)} fusion(bf16[1,768,1536]{2,1,0:T(8,128)(2,1)} %param.20, bf16[192,768]{1,0:T(8,128)(2,1)S(1)} %gather_fusion.1, pred[192]{0:T(512)(128)(4,1)S(1)} %compare_and_fusion.1), kind=kOutput, calls=%fused_computation.34 | convolution fusion | flops 453427200 | bytes 3244224 | tf_op jit(solution)/shard_map/dot_general | solution.py:109
  133.1 0.9 copy.25
  134.1 0.9 copy.27
  135.0 5.1 %fusion.101 = (f32[12,512]{1,0:T(8,128)S(1)}, f32[12,512,192]{1,2,0:T(8,128)}) fusion(bf16[512,12,64]{0,2,1:T(8,128)(2,1)} %bitcast.102, bf16[192,12,64]{0,2,1:T(8,128)(2,1)} %bitcast.108), kind=kOutput, calls=%fused_computation.123 | convolution fusion | flops 154534080 | bytes 5824512 | tf_op jit(solution)/shard_map/while/body/eval_jaxpr/sub | solution.py:45
  140.1 3.8 %fusion.40 = bf16[12,64,512]{2,1,0:T(8,128)(2,1)} fusion(bf16[192,12,64]{0,2,1:T(8,128)(2,1)S(1)} %bitcast.106, f32[12,512,192]{1,2,0:T(8,128)} %get-tuple-element.31, f32[12,512]{1,0:T(8,128)S(1)} %get-tuple-element.30), kind=kOutput, calls=%fused_computation.46 | convolution fusion | flops 153747456 | bytes 5824512 | tf_op jit(solution)/shard_map/while/body/eval_jaxpr/hqk,khe->qhe/dot_general | solution.py:46
  143.9 1.1 fusion.99
  145.0 0.2 copy.28
  145.2 0.9 copy.29
  146.1 5.0 %fusion.100 = (f32[12,512]{1,0:T(8,128)S(1)}, f32[12,512,192]{1,2,0:T(8,128)}) fusion(bf16[512,12,64]{0,2,1:T(8,128)(2,1)} %bitcast.103, bf16[192,12,64]{0,2,1:T(8,128)(2,1)} %bitcast.107), kind=kOutput, calls=%fused_computation.122 | convolution fusion | flops 154534080 | bytes 5824512 | tf_op jit(solution)/shard_map/while/body/eval_jaxpr/sub | solution.py:45
  151.1 3.0 %fusion.39 = bf16[12,64,512]{2,1,0:T(8,128)(2,1)S(1)} fusion(bf16[192,12,64]{0,2,1:T(8,128)(2,1)S(1)} %bitcast.105, f32[12,512,192]{1,2,0:T(8,128)} %get-tuple-element.29, f32[12,512]{1,0:T(8,128)S(1)} %get-tuple-element.28), kind=kOutput, calls=%fused_computation.45 | convolution fusion | flops 153747456 | bytes 5824512 | tf_op jit(solution)/shard_map/while/body/eval_jaxpr/hqk,khe->qhe/dot_general | solution.py:46
  154.1 2.3 %fusion.46 = bf16[1,512,768]{2,1,0:T(8,128)(2,1)} fusion(bf16[1,1536,768]{2,1,0:T(8,128)(2,1)S(1)} %copy-done, bf16[512,768]{0,1:T(8,128)(2,1)S(1)} %bitcast.112, bf16[512,768]{0,1:T(8,128)(2,1)S(1)} %bitcast.111), kind=kOutput, calls=%fused_computation.49 | convolution fusion | flops 1211498496 | bytes 4718592 | tf_op jit(solution)/shard_map/dot_general | solution.py:130
  (35 shorter events, 1.0 us)
Async XLA Ops:
  0.0 154.1 %copy-start = (bf16[1,1536,768]{2,1,0:T(8,128)(2,1)S(1)}, bf16[1,1536,768]{2,1,0:T(8,128)(2,1)}, u32[]{:S(2)}) copy-start(bf16[1,1536,768]{2,1,0:T(8,128)(2,1)} %param.21) | copy-start | bytes 7077892
  23.5 7.5 %copy-start.2 = (bf16[1,32,768]{2,1,0:T(8,128)(2,1)S(1)}, bf16[1,32,768]{2,1,0:T(8,128)(2,1)}, u32[]{:S(2)}) copy-start(bf16[1,32,768]{2,1,0:T(8,128)(2,1)} %param.13) | copy-start | bytes 147460
  74.4 17.3 %copy-start.3 = (s32[1,192]{1,0:T(1,128)S(1)}, s32[1,192]{1,0:T(1,128)}, u32[]{:S(2)}) copy-start(s32[1,192]{1,0:T(1,128)} %param.16) | copy-start | bytes 2308
  85.5 12.8 %all-to-all-start = ((bf16[8,8,768]{2,1,0:T(8,128)(2,1)}), bf16[8,8,768]{2,1,0:T(8,128)(2,1)S(1)}, u32[]{:S(2)}, u32[]{:S(2)}) async-start(bf16[8,8,768]{2,1,0:T(8,128)(2,1)} %bitcast.15), calls=%async_computation | async-start | bytes 196608 | tf_op jit(solution)/shard_map/all_to_all | solution.py:98
  133.0 10.9 %collective-permute-start = (bf16[192,1536]{1,0:T(8,128)(2,1)S(1)}, bf16[192,1536]{1,0:T(8,128)(2,1)}, u32[]{:S(2)}, u32[]{:S(2)}) collective-permute-start(bf16[192,1536]{1,0:T(8,128)(2,1)S(1)} %convolution_convert_fusion.1), channel_id=1, source_target_pairs={{0,1},{1,0},{2,3},{3,2},{4,5},{5,4},{6,7},{7,6},{8,9},{9,8},{10,11... | collective-permute-start | bytes 1769480 | tf_op jit(solution)/shard_map/ppermute | solution.py:20
  135.0 5.1 %copy-start.1 = (bf16[192,768]{0,1:T(8,128)(2,1)S(1)}, bf16[192,768]{0,1:T(8,128)(2,1)}, u32[]{:S(2)}) copy-start(bf16[192,768]{0,1:T(8,128)(2,1)} %copy.25) | copy-start | bytes 884740
  151.1 3.0 %copy-start.4 = (bf16[12,64,512]{2,1,0:T(8,128)(2,1)S(1)}, bf16[12,64,512]{2,1,0:T(8,128)(2,1)}, u32[]{:S(2)}) copy-start(bf16[12,64,512]{2,1,0:T(8,128)(2,1)} %fusion.40) | copy-start | bytes 2359300
where the time goes:
time: 157 us; the launch traced here: 156 us
  blocking collectives  63.9 us (41%)
  matrix products  53.9 us (34%)
  local copies, waits for them, and re-layouts  25.6 us (16%)
  starting transfers between devices  5.73 us (4%)
  other arithmetic  3.97 us (3%)
  waiting for transfers between devices  3.17 us (2%)
    all_gather x1, blocking collectives, per_device(): all_queries = lax.all_gather(own_queries, 'pts', axis=0, tiled=True)  32.9 us
    all_gather x1, blocking collectives, per_device(): all_nodes = lax.all_gather(node_feat, 'pts', axis=0, tiled=True)  31 us
    dot_general x1, matrix products, per_device(): jnp.dot(hidden, w_mid[0], preferred_element_type=jnp.float32)  11.2 us
    sub x2, matrix products, attend(): weights = jax.nn.softmax(scores, axis=-1).astype(jnp.bfloat16)  10.1 us
    dot_general x1, matrix products, pool_blocks(): jnp.einsum('nhr,nrhe->nhe', weights, split_rows, preferred_element_type=j...  9.46 us
    dot_general x1, matrix products, pool_blocks(): jnp.einsum('nrhe,nhe->nhr', split_rows, asked_rows, preferred_element_typ...  9.18 us
    convert_element_type x1, local copies, waits for them, and re-layouts, per_device(): jnp.dot(hidden, w_mid[0], preferred_element_type=jnp.float32)  8.75 us
    unnamed x12, local copies, waits for them, and re-layouts  8.03 us
  transfers between devices with their start and end apart: 2, of which 1 were waited for; matrix products, arithmetic and copies ran while one was open for 9% of the time, Pallas kernels for 0%

commit v1 on v0

v1 whole, which is shorter than its diff:
```python
import functools
import math

import jax
import jax.numpy as jnp
from jax import lax
from jax.experimental import pallas as pl
from jax.experimental.pallas import tpu as pltpu
from jax.sharding import PartitionSpec as P

D = 768
HEADS = 12
BLK = 128
HS = D // HEADS
LANES = 128
HP = 16
BF = jnp.bfloat16
F32 = jnp.float32
MESH = pl.DeviceIdType.MESH


def nn(a, b):
    return lax.dot_general(a, b, (((1,), (0,)), ((), ())), preferred_element_type=F32)


def nt(a, b):
    return lax.dot_general(a, b, (((1,), (1,)), ((), ())), preferred_element_type=F32)


def iota(shape, axis):
    return lax.broadcasted_iota(jnp.int32, shape, axis)


def kernel(
    shards,
    sq_ref,
    owner_ref,
    slot_ref,
    anchor_ref,
    w_in_ref,
    pf_hbm,
    qf_hbm,
    w_q_hbm,
    w_mid_hbm,
    w_kv_hbm,
    w_out_hbm,
    out_ref,
    pf,
    qf,
    w_q,
    w_mid,
    w_kv,
    w_out,
    hid,
    queries,
    all_q,
    all_p,
    u_s,
    s_s,
    g_s,
    kv_own,
    kv_far,
    joined,
    load_sem,
    q_send,
    q_recv,
    p_send,
    p_recv,
    kv_send,
    kv_recv,
):
    me = lax.axis_index("pts")
    br = lax.axis_index("branch")
    nodes_here = sq_ref.shape[0]
    node_total = shards * nodes_here
    block_total = owner_ref.shape[1]
    nb = block_total // shards
    anchors = anchor_ref.shape[1]
    half = nb // 2

    loads = []
    for i, (src, dst) in enumerate(
        ((pf_hbm, pf), (qf_hbm, qf), (w_q_hbm, w_q), (w_mid_hbm, w_mid), (w_kv_hbm, w_kv), (w_out_hbm, w_out))
    ):
        copy = pltpu.make_async_copy(src, dst, load_sem.at[i])
        copy.start()
        loads.append(copy)

    barrier = pltpu.get_barrier_semaphore()
    for k in range(1, shards):
        pl.semaphore_signal(
            barrier, inc=1, device_id={"pts": lax.rem(me + k, shards)}, device_id_type=MESH
        )
    pl.semaphore_signal(barrier, inc=1, device_id={"branch": 1 - br}, device_id_type=MESH)
    pl.semaphore_wait(barrier, shards)

    def q_copy(k, row):
        place = all_q.at[pl.ds(pl.multiple_of(row * nodes_here, nodes_here), nodes_here)]
        return pltpu.make_async_remote_copy(
            src_ref=sq_ref,
            dst_ref=place,
            send_sem=q_send.at[k],
            recv_sem=q_recv.at[row],
            device_id={"pts": lax.rem(me + k, shards)},
            device_id_type=MESH,
        )

    def p_copy(c, k, row):
        place = all_p.at[pl.ds(pl.multiple_of(row * nb + c * half, half), half)]
        return pltpu.make_async_remote_copy(
            src_ref=place,
            dst_ref=place,
            send_sem=p_send.at[c, k],
            recv_sem=p_recv.at[c, row],
            device_id={"pts": lax.rem(me + k, shards)},
            device_id_type=MESH,
        )

    for k in range(1, shards):
        q_copy(k, me).start()
    all_q[pl.ds(pl.multiple_of(me * nodes_here, nodes_here), nodes_here), :] = sq_ref[...]

    w_half = w_in_ref[...] * jnp.asarray(0.5, BF)
    gain = math.sqrt(2.0 / math.pi)
    loads[0].wait()
    rows = 512

    def encode(i, carry):
        at = pl.ds(pl.multiple_of(i * rows, rows), rows)
        y = nn(pf[at, :], w_half)
        t = jnp.tanh(y * (2.0 * gain + (8.0 * 0.044715 * gain) * (y * y)))
        hid[at, :] = (y + y * t).astype(BF)
        return carry

    lax.fori_loop(0, nb * BLK // rows, encode, 0)

    loads[1].wait()
    loads[2].wait()
    scale = math.log2(math.e) / math.sqrt(HS)
    queries[...] = (nn(qf[...], w_q[...]) * scale).astype(BF)

    ids_row = owner_ref[...] * nodes_here + slot_ref[...]
    my_ids = jnp.sum(
        jnp.where(
            iota((nb, block_total), 1) == iota((nb, block_total), 0) + me * nb, ids_row, 0
        ).astype(F32),
        axis=1,
        keepdims=True,
    ).astype(jnp.int32)
    anchor_col = jnp.sum(
        jnp.where(
            iota((anchors, anchors), 1) == iota((anchors, anchors), 0), anchor_ref[...], 0
        ).astype(F32),
        axis=1,
        keepdims=True,
    ).astype(jnp.int32)
    pick_block = (iota((nb, node_total), 1) == my_ids).astype(F32).astype(BF)

    loads[3].wait()
    for k in range(1, shards):
        q_copy(k, lax.rem(me + shards - k, shards)).wait_recv()

    block_q = nn(pick_block, all_q[...])
    own_head = iota((HP, D), 1) // HS == iota((HP, D), 0)
    for c in range(2):
        asked = jnp.where(
            own_head[None], block_q[c * half : (c + 1) * half][:, None, :], 0.0
        ).reshape(half * HP, D)
        u_s[...] = (nt(asked.astype(BF), w_mid[...]) / math.sqrt(HS)).astype(BF)
        for n in range(half):
            rows_n = hid[pl.ds((c * half + n) * BLK, BLK), :]
            s_s[pl.ds(n * HP, HP), :] = nt(u_s[pl.ds(n * HP, HP), :], rows_n)
        scores = s_s[...]
        e = jnp.exp(scores - jnp.max(scores, axis=1, keepdims=True))
        weights = (e / jnp.sum(e, axis=1, keepdims=True)).astype(BF)
        for n in range(half):
            rows_n = hid[pl.ds((c * half + n) * BLK, BLK), :]
            g_s[pl.ds(n * HP, HP), :] = nn(weights[n * HP : (n + 1) * HP], rows_n).astype(BF)
        mixed = nn(g_s[...], w_mid[...]).reshape(half, HP, D)
        pooled = jnp.sum(jnp.where(own_head[None], mixed, 0.0), axis=1).astype(BF)
        all_p[pl.ds(pl.multiple_of(me * nb + c * half, half), half), :] = pooled
        for k in range(1, shards):
            p_copy(c, k, me).start()

    member = (anchor_col == ids_row).astype(F32)
    count = jnp.sum(member, axis=1, keepdims=True)
    pick_node = (iota((anchors, node_total), 1) == anchor_col).astype(F32).astype(BF)
    anchor_q = nn(pick_node, all_q[...])
    loads[4].wait()
    for c in range(2):
        for k in range(1, shards):
            p_copy(c, k, lax.rem(me + shards - k, shards)).wait_recv()
    pooled_sum = nn(member.astype(BF), all_p[...])
    v = anchor_q + pooled_sum / jnp.maximum(count, 1.0)
    feat = (v * lax.rsqrt(jnp.mean(v * v, axis=1, keepdims=True) + 1e-06)).astype(BF)
    kv_own[...] = nn(feat, w_kv[...]).astype(BF)
    swap = pltpu.make_async_remote_copy(
        src_ref=kv_own,
        dst_ref=kv_far,
        send_sem=kv_send,
        recv_sem=kv_recv,
        device_id={"branch": 1 - br},
        device_id_type=MESH,
    )
    swap.start()

    lane = iota((anchors, LANES), 1) // HS

    def attend(kv, base):
        for g in range(D // LANES):
            at = pl.ds(g * LANES, LANES)
            q = queries[:, at]
            keys = kv[:, at]
            values = kv[:, pl.ds(D + g * LANES, LANES)]
            total = None
            for h in range(LANES // HS):
                mine = lane == h
                zero = jnp.zeros_like(keys)
                s = nt(q, jnp.where(mine, keys, zero))
                p = jnp.exp2(s - jnp.max(s, axis=1, keepdims=True)).astype(BF)
                wide = jnp.concatenate(
                    [jnp.where(mine, values, zero), jnp.where(mine, 1.0, 0.0).astype(BF)], axis=1
                )
                part = nn(p, wide)
                total = part if total is None else total + part
            joined[:, pl.ds(base + g * LANES, LANES)] = (
                total[:, :LANES] / total[:, LANES:]
            ).astype(BF)

    attend(kv_own, 0)
    swap.wait()
    attend(kv_far, D)
    loads[5].wait()
    out_ref[...] = nn(joined[...], w_out[...]).astype(BF)

    for k in range(1, shards):
        q_copy(k, me).wait_send()
        for c in range(2):
            p_copy(c, k, me).wait_send()


def per_device(
    point_feat,
    query_feat,
    supernode_query,
    route_owner,
    route_slot,
    anchor_index,
    w_in,
    w_mid,
    w_q,
    w_kv,
    w_out,
):
    shards = lax.axis_size("pts")
    points = point_feat[0]
    rows = query_feat.shape[1]
    nodes = supernode_query.shape[1] * shards
    blocks = route_slot.shape[1]
    half = blocks // shards // 2
    anchors = anchor_index.shape[1]
    vmem = pl.BlockSpec(memory_space=pltpu.VMEM)
    hbm = pl.BlockSpec(memory_space=pl.ANY)
    result = pl.pallas_call(
        functools.partial(kernel, shards),
        out_shape=jax.ShapeDtypeStruct((rows, D), BF),
        in_specs=[vmem] * 5 + [hbm] * 6,
        out_specs=vmem,
        scratch_shapes=[
            pltpu.VMEM(points.shape, BF),
            pltpu.VMEM((rows, D), BF),
            pltpu.VMEM((D, D), BF),
            pltpu.VMEM((D, D), BF),
            pltpu.VMEM((D, 2 * D), BF),
            pltpu.VMEM((2 * D, D), BF),
            pltpu.VMEM((points.shape[0], D), BF),
            pltpu.VMEM((rows, D), BF),
            pltpu.VMEM((nodes, D), BF),
            pltpu.VMEM((blocks, D), BF),
            pltpu.VMEM((half * HP, D), BF),
            pltpu.VMEM((half * HP, BLK), F32),
            pltpu.VMEM((half * HP, D), BF),
            pltpu.VMEM((anchors, 2 * D), BF),
            pltpu.VMEM((anchors, 2 * D), BF),
            pltpu.VMEM((rows, 2 * D), BF),
            pltpu.SemaphoreType.DMA((6,)),
            pltpu.SemaphoreType.DMA((shards,)),
            pltpu.SemaphoreType.DMA((shards,)),
            pltpu.SemaphoreType.DMA((2, shards)),
            pltpu.SemaphoreType.DMA((2, shards)),
            pltpu.SemaphoreType.DMA,
            pltpu.SemaphoreType.DMA,
        ],
        compiler_params=pltpu.CompilerParams(
            collective_id=0, has_side_effects=True, vmem_limit_bytes=48 * 1024 * 1024
        ),
    )(
        supernode_query[0],
        route_owner[0].reshape(1, blocks),
        route_slot,
        anchor_index,
        w_in[0],
        points,
        query_feat[0],
        w_q[0],
        w_mid[0],
        w_kv[0],
        w_out[0],
    )
    return result[None]


def solution(mesh):
    return jax.shard_map(
        per_device,
        mesh=mesh,
        in_specs=(
            P("branch", ("groups", "pts"), None),
            P("branch", ("groups", "pts"), None),
            P("branch", ("groups", "pts"), None),
            P("branch", "groups", None),
            P("branch", "groups"),
            P("branch", "groups"),
            P("branch", None, None),
            P("branch", None, None),
            P("branch", None, None),
            P("branch", None, None),
            P("branch", None, None),
        ),
        out_specs=P("branch", ("groups", "pts"), None),
        check_vma=False,
    )
```

time: 157 us -> 44.2 us (0.28)
  blocking collectives: 63.9 us -> 0 us
  matrix products: 53.9 us -> 0 us
  Pallas kernels: 0 us -> 34.2 us
  local copies, waits for them, and re-layouts: 25.6 us -> 9.54 us
  starting transfers between devices: 5.73 us -> 0 us
  other arithmetic: 3.97 us -> 0 us
  waiting for transfers between devices: 3.17 us -> 0 us
    all_gather x2 -> x0, blocking collectives: 63.9 us -> none  [the longest x1 32.9 us: per_device(): all_queries = lax.all_gather(own_queries, 'pts', axis=0, tiled=True)]
    dot_general x9 -> x0, matrix products: 43.8 us -> none  [the longest x1 11.2 us: per_device(): jnp.dot(hidden, w_mid[0], preferred_element_type=jnp.float32)]
    pallas_call x0 -> x1, Pallas kernels: none -> 34.2 us  [per_device(): pl.pallas_call(functools.partial(kernel, shards), out_shape=jax.ShapeDtyp...]
    sub x2 -> x0, matrix products: 10.1 us -> none  [attend(): weights = jax.nn.softmax(scores, axis=-1).astype(jnp.bfloat16)]
    convert_element_type x2 -> x0, local copies, waits for them, and re-layouts: 9.91 us -> none  [the longest x1 8.75 us: per_device(): jnp.dot(hidden, w_mid[0], preferred_element_type=jnp.float32)]
    all_to_all x1 -> x0, starting transfers between devices: 5.66 us -> none  [per_device(): lax.all_to_all(outgoing, 'pts', split_axis=0, concat_axis=0, tiled=True)]
    slice x6 -> x0, local copies, waits for them, and re-layouts: 4.11 us -> none  [the longest x2 2.04 us: answer(): partner_kv[:, :model_width]]
    all_to_all x1 -> x0, waiting for transfers between devices: 3.17 us -> none  [per_device(): lax.all_to_all(outgoing, 'pts', split_axis=0, concat_axis=0, tiled=True)]
  transfers between devices with their start and end apart: 2 -> 0, of which waited for: 1 -> 0; matrix products, arithmetic and copies ran while one was open for 9% -> 0% of each run, Pallas kernels for 0% -> 0%
where the time goes in v1:
time: 44.2 us; the launch traced here: 43.8 us
  Pallas kernels  34.2 us (77%)
  local copies, waits for them, and re-layouts  9.54 us (22%)
    pallas_call x1, Pallas kernels, per_device(): pl.pallas_call(functools.partial(kernel, shards), out_shape=jax.ShapeDtyp...  34.2 us
    unnamed x19, local copies, waits for them, and re-layouts  9.54 us

profile of v1, /device:TPU:0, one launch (start us, length us, event | category | flops | bytes accessed | tf_op | source)
XLA Modules:
  0.0 43.8 jit_solution(7106612320237630565)
XLA Ops:
  0.0 0.0 copy-start
  0.0 1.3 %copy-done = bf16[1,768,768]{2,1,0:T(8,128)(2,1)S(1)} copy-done((bf16[1,768,768]{2,1,0:T(8,128)(2,1)S(1)}, bf16[1,768,768]{2,1,0:T(8,128)(2,1)}, u32[]{:S(2)}) %copy-start) | copy-done | bytes 1179672
  1.3 0.0 copy-start.1
  1.3 1.3 %copy-done.1 = bf16[1,768,768]{2,1,0:T(8,128)(2,1)S(1)} copy-done((bf16[1,768,768]{2,1,0:T(8,128)(2,1)S(1)}, bf16[1,768,768]{2,1,0:T(8,128)(2,1)}, u32[]{:S(2)}) %copy-start.1) | copy-done | bytes 1179672
  2.5 0.0 copy-start.2
  2.5 1.2 %copy-done.2 = bf16[1,4096,128]{2,1,0:T(8,128)(2,1)S(1)} copy-done((bf16[1,4096,128]{2,1,0:T(8,128)(2,1)S(1)}, bf16[1,4096,128]{2,1,0:T(8,128)(2,1)}, u32[]{:S(2)}) %copy-start.2) | copy-done | bytes 1048600
  3.8 0.0 copy-start.3
  3.8 1.1 %copy-done.3 = bf16[1,512,768]{2,1,0:T(8,128)(2,1)S(1)} copy-done((bf16[1,512,768]{2,1,0:T(8,128)(2,1)S(1)}, bf16[1,512,768]{2,1,0:T(8,128)(2,1)}, u32[]{:S(2)}) %copy-start.3) | copy-done | bytes 786456
  4.9 0.0 copy-start.4
  4.9 0.9 %copy-done.4 = bf16[1,128,768]{2,1,0:T(8,128)(2,1)S(1)} copy-done((bf16[1,128,768]{2,1,0:T(8,128)(2,1)S(1)}, bf16[1,128,768]{2,1,0:T(8,128)(2,1)}, u32[]{:S(2)}) %copy-start.4) | copy-done | bytes 196632
  5.8 0.0 copy-start.5
  5.8 0.8 %copy-done.5 = bf16[1,32,768]{2,1,0:T(8,128)(2,1)S(1)} copy-done((bf16[1,32,768]{2,1,0:T(8,128)(2,1)S(1)}, bf16[1,32,768]{2,1,0:T(8,128)(2,1)}, u32[]{:S(2)}) %copy-start.5) | copy-done | bytes 49176
  6.6 0.0 copy-start.6
  6.6 0.7 %copy-done.6 = s32[1,256,1]{1,2,0:T(1,128)S(1)} copy-done((s32[1,256,1]{1,2,0:T(1,128)S(1)}, s32[1,256,1]{1,2,0:T(1,128)}, u32[]{:S(2)}) %copy-start.6) | copy-done | bytes 1048
  7.3 0.0 copy-start.7
  7.3 0.7 %copy-done.7 = s32[1,256]{1,0:T(1,128)S(1)} copy-done((s32[1,256]{1,0:T(1,128)S(1)}, s32[1,256]{1,0:T(1,128)}, u32[]{:S(2)}) %copy-start.7) | copy-done | bytes 1048
  8.0 0.0 copy-start.8
  8.0 0.7 %copy-done.8 = s32[1,192]{1,0:T(1,128)S(1)} copy-done((s32[1,192]{1,0:T(1,128)S(1)}, s32[1,192]{1,0:T(1,128)}, u32[]{:S(2)}) %copy-start.8) | copy-done | bytes 792
  8.7 34.2 %shard_map.109 = bf16[512,768]{1,0:T(8,128)(2,1)S(1)} custom-call(bf16[32,768]{1,0:T(8,128)(2,1)S(1)} %bitcast.16, s32[1,256]{1,0:T(1,128)S(1)} %bitcast.17, s32[1,256]{1,0:T(1,128)S(1)} %copy-done.7, s32[1,192]{1,0:T(1,128)S(1)} %copy-done.8, bf16[128,768]{1,0:T(8,128)(2,1)S(1)} %bitcast.15, bf16[4096,128]{1,0:T(8,128)(2,1)S(1)} %bitcast.13, ...), custom_call_target="tpu_custom_call" | custom-call | tf_op jit(solution)/shard_map/pallas_call | solution.py:264
  42.9 0.9 %copy.13 = bf16[1,512,768]{2,1,0:T(8,128)(2,1)} copy(bf16[1,512,768]{2,1,0:T(8,128)(2,1)S(1)} %bitcast.10) | data formatting | bytes 1572864
Async XLA Ops:
  0.0 1.3 %copy-start = (bf16[1,768,768]{2,1,0:T(8,128)(2,1)S(1)}, bf16[1,768,768]{2,1,0:T(8,128)(2,1)}, u32[]{:S(2)}) copy-start(bf16[1,768,768]{2,1,0:T(8,128)(2,1)} %param.19) | copy-start | bytes 3538948
  1.3 1.3 %copy-start.1 = (bf16[1,768,768]{2,1,0:T(8,128)(2,1)S(1)}, bf16[1,768,768]{2,1,0:T(8,128)(2,1)}, u32[]{:S(2)}) copy-start(bf16[1,768,768]{2,1,0:T(8,128)(2,1)} %param.18) | copy-start | bytes 3538948
  2.5 1.2 %copy-start.2 = (bf16[1,4096,128]{2,1,0:T(8,128)(2,1)S(1)}, bf16[1,4096,128]{2,1,0:T(8,128)(2,1)}, u32[]{:S(2)}) copy-start(bf16[1,4096,128]{2,1,0:T(8,128)(2,1)} %param.11) | copy-start | bytes 3145732
  3.8 1.1 %copy-start.3 = (bf16[1,512,768]{2,1,0:T(8,128)(2,1)S(1)}, bf16[1,512,768]{2,1,0:T(8,128)(2,1)}, u32[]{:S(2)}) copy-start(bf16[1,512,768]{2,1,0:T(8,128)(2,1)} %param.12) | copy-start | bytes 2359300
  4.9 0.9 %copy-start.4 = (bf16[1,128,768]{2,1,0:T(8,128)(2,1)S(1)}, bf16[1,128,768]{2,1,0:T(8,128)(2,1)}, u32[]{:S(2)}) copy-start(bf16[1,128,768]{2,1,0:T(8,128)(2,1)} %param.17) | copy-start | bytes 589828
  5.8 0.8 %copy-start.5 = (bf16[1,32,768]{2,1,0:T(8,128)(2,1)S(1)}, bf16[1,32,768]{2,1,0:T(8,128)(2,1)}, u32[]{:S(2)}) copy-start(bf16[1,32,768]{2,1,0:T(8,128)(2,1)} %param.13) | copy-start | bytes 147460
  6.6 0.7 %copy-start.6 = (s32[1,256,1]{1,2,0:T(1,128)S(1)}, s32[1,256,1]{1,2,0:T(1,128)}, u32[]{:S(2)}) copy-start(s32[1,256,1]{1,2,0:T(1,128)} %param.14) | copy-start | bytes 3076
  7.3 0.7 %copy-start.7 = (s32[1,256]{1,0:T(1,128)S(1)}, s32[1,256]{1,0:T(1,128)}, u32[]{:S(2)}) copy-start(s32[1,256]{1,0:T(1,128)} %slot_ref.1) | copy-start | bytes 3076
  8.0 0.7 %copy-start.8 = (s32[1,192]{1,0:T(1,128)S(1)}, s32[1,192]{1,0:T(1,128)}, u32[]{:S(2)}) copy-start(s32[1,192]{1,0:T(1,128)} %anchor_ref.1) | copy-start | bytes 2308

commit v2 on v1

--- a/solution.py
+++ b/solution.py
@@ -33,11 +33,11 @@
 
 def kernel(
     shards,
-    sq_ref,
-    owner_ref,
-    slot_ref,
-    anchor_ref,
-    w_in_ref,
+    sq_hbm,
+    owner_hbm,
+    slot_hbm,
+    anchor_hbm,
+    w_in_hbm,
     pf_hbm,
     qf_hbm,
     w_q_hbm,
@@ -45,6 +45,11 @@
     w_kv_hbm,
     w_out_hbm,
     out_ref,
+    sq_ref,
+    owner_ref,
+    slot_ref,
+    anchor_ref,
+    w_in_ref,
     pf,
     qf,
     w_q,
@@ -80,7 +85,19 @@
 
     loads = []
     for i, (src, dst) in enumerate(
-        ((pf_hbm, pf), (qf_hbm, qf), (w_q_hbm, w_q), (w_mid_hbm, w_mid), (w_kv_hbm, w_kv), (w_out_hbm, w_out))
+        (
+            (sq_hbm, sq_ref),
+            (w_in_hbm, w_in_ref),
+            (owner_hbm, owner_ref),
+            (slot_hbm, slot_ref),
+            (anchor_hbm, anchor_ref),
+            (pf_hbm, pf),
+            (qf_hbm, qf),
+            (w_q_hbm, w_q),
+            (w_mid_hbm, w_mid),
+            (w_kv_hbm, w_kv),
+            (w_out_hbm, w_out),
+        )
     ):
         copy = pltpu.make_async_copy(src, dst, load_sem.at[i])
         copy.start()
@@ -116,13 +133,15 @@
             device_id_type=MESH,
         )
 
+    loads[0].wait()
     for k in range(1, shards):
         q_copy(k, me).start()
     all_q[pl.ds(pl.multiple_of(me * nodes_here, nodes_here), nodes_here), :] = sq_ref[...]
 
+    loads[1].wait()
     w_half = w_in_ref[...] * jnp.asarray(0.5, BF)
     gain = math.sqrt(2.0 / math.pi)
-    loads[0].wait()
+    loads[5].wait()
     rows = 512
 
     def encode(i, carry):
@@ -134,11 +153,13 @@
 
     lax.fori_loop(0, nb * BLK // rows, encode, 0)
 
-    loads[1].wait()
-    loads[2].wait()
+    loads[6].wait()
+    loads[7].wait()
     scale = math.log2(math.e) / math.sqrt(HS)
     queries[...] = (nn(qf[...], w_q[...]) * scale).astype(BF)
 
+    for i in (2, 3, 4):
+        loads[i].wait()
     ids_row = owner_ref[...] * nodes_here + slot_ref[...]
     my_ids = jnp.sum(
         jnp.where(
@@ -156,7 +177,7 @@
     ).astype(jnp.int32)
     pick_block = (iota((nb, node_total), 1) == my_ids).astype(F32).astype(BF)
 
-    loads[3].wait()
+    loads[8].wait()
     for k in range(1, shards):
         q_copy(k, lax.rem(me + shards - k, shards)).wait_recv()
 
@@ -186,7 +207,7 @@
     count = jnp.sum(member, axis=1, keepdims=True)
     pick_node = (iota((anchors, node_total), 1) == anchor_col).astype(F32).astype(BF)
     anchor_q = nn(pick_node, all_q[...])
-    loads[4].wait()
+    loads[9].wait()
     for c in range(2):
         for k in range(1, shards):
             p_copy(c, k, lax.rem(me + shards - k, shards)).wait_recv()
@@ -230,7 +251,7 @@
     attend(kv_own, 0)
     swap.wait()
     attend(kv_far, D)
-    loads[5].wait()
+    loads[10].wait()
     out_ref[...] = nn(joined[...], w_out[...]).astype(BF)
 
     for k in range(1, shards):
@@ -260,13 +281,18 @@
     half = blocks // shards // 2
     anchors = anchor_index.shape[1]
     vmem = pl.BlockSpec(memory_space=pltpu.VMEM)
-    hbm = pl.BlockSpec(memory_space=pl.ANY)
+    hbm = pl.BlockSpec(memory_space=pltpu.HBM)
     result = pl.pallas_call(
         functools.partial(kernel, shards),
         out_shape=jax.ShapeDtypeStruct((rows, D), BF),
-        in_specs=[vmem] * 5 + [hbm] * 6,
+        in_specs=[hbm] * 11,
         out_specs=vmem,
         scratch_shapes=[
+            pltpu.VMEM(supernode_query.shape[1:], BF),
+            pltpu.VMEM((1, blocks), jnp.int32),
+            pltpu.VMEM((1, blocks), jnp.int32),
+            pltpu.VMEM((1, anchors), jnp.int32),
+            pltpu.VMEM(w_in.shape[1:], BF),
             pltpu.VMEM(points.shape, BF),
             pltpu.VMEM((rows, D), BF),
             pltpu.VMEM((D, D), BF),
@@ -283,7 +309,7 @@
             pltpu.VMEM((anchors, 2 * D), BF),
             pltpu.VMEM((anchors, 2 * D), BF),
             pltpu.VMEM((rows, 2 * D), BF),
-            pltpu.SemaphoreType.DMA((6,)),
+            pltpu.SemaphoreType.DMA((11,)),
             pltpu.SemaphoreType.DMA((shards,)),
             pltpu.SemaphoreType.DMA((shards,)),
             pltpu.SemaphoreType.DMA((2, shards)),
@@ -292,7 +318,7 @@
             pltpu.SemaphoreType.DMA,
         ],
         compiler_params=pltpu.CompilerParams(
-            collective_id=0, has_side_effects=True, vmem_limit_bytes=48 * 1024 * 1024
+            collective_id=0, has_side_effects=True, vmem_limit_bytes=60 * 1024 * 1024
         ),
     )(
         supernode_query[0],

time: 44.2 us -> 36.9 us (0.83)
  local copies, waits for them, and re-layouts: 9.54 us -> 2.06 us
  Pallas kernels: 34.2 us -> 34.7 us
    unnamed x19 -> x1, local copies, waits for them, and re-layouts: 9.54 us -> 2.06 us
where the time goes in v2:
time: 36.9 us; the launch traced here: 36.8 us
  Pallas kernels  34.7 us (94%)
  local copies, waits for them, and re-layouts  2.06 us (6%)
    pallas_call x1, Pallas kernels, per_device(): pl.pallas_call(functools.partial(kernel, shards), out_shape=jax.ShapeDtyp...  34.7 us
    unnamed x1, local copies, waits for them, and re-layouts  2.06 us

profile of v2, /device:TPU:0, one launch (start us, length us, event | category | flops | bytes accessed | tf_op | source)
XLA Modules:
  0.0 36.8 jit_solution(16302219858630399478)
XLA Ops:
  0.0 34.7 %shard_map.109 = bf16[512,768]{1,0:T(8,128)(2,1)} custom-call(bf16[32,768]{1,0:T(8,128)(2,1)} %bitcast.18, s32[1,256]{1,0:T(1,128)} %bitcast.19, s32[1,256]{1,0:T(1,128)} %slot_hbm.1, s32[1,192]{1,0:T(1,128)} %anchor_hbm.1, bf16[128,768]{1,0:T(8,128)(2,1)} %bitcast.17, bf16[4096,128]{1,0:T(8,128)(2,1)} %bitcast.15, bf16[512,768]{1,0:T(8,128)(2,1)} %bitcast.16, ...), custom_call_target="tpu_custom_call" | custom-call | tf_op jit(solution)/shard_map/pallas_call | solution.py:285
  34.7 2.1 %copy.13 = bf16[1,512,768]{2,1,0:T(8,128)(2,1)} copy(bf16[1,512,768]{2,1,0:T(8,128)(2,1)} %bitcast.10) | data formatting | bytes 1572864

commit v3 on v2

--- a/solution.py
+++ b/solution.py
@@ -43,8 +43,7 @@
     w_q_hbm,
     w_mid_hbm,
     w_kv_hbm,
-    w_out_hbm,
-    out_ref,
+    joined,
     sq_ref,
     owner_ref,
     slot_ref,
@@ -55,7 +54,6 @@
     w_q,
     w_mid,
     w_kv,
-    w_out,
     hid,
     queries,
     all_q,
@@ -65,7 +63,6 @@
     g_s,
     kv_own,
     kv_far,
-    joined,
     load_sem,
     q_send,
     q_recv,
@@ -96,7 +93,6 @@
             (w_q_hbm, w_q),
             (w_mid_hbm, w_mid),
             (w_kv_hbm, w_kv),
-            (w_out_hbm, w_out),
         )
     ):
         copy = pltpu.make_async_copy(src, dst, load_sem.at[i])
@@ -152,11 +148,6 @@
         return carry
 
     lax.fori_loop(0, nb * BLK // rows, encode, 0)
-
-    loads[6].wait()
-    loads[7].wait()
-    scale = math.log2(math.e) / math.sqrt(HS)
-    queries[...] = (nn(qf[...], w_q[...]) * scale).astype(BF)
 
     for i in (2, 3, 4):
         loads[i].wait()
@@ -207,6 +198,11 @@
     count = jnp.sum(member, axis=1, keepdims=True)
     pick_node = (iota((anchors, node_total), 1) == anchor_col).astype(F32).astype(BF)
     anchor_q = nn(pick_node, all_q[...])
+    loads[6].wait()
+    loads[7].wait()
+    scale = math.log2(math.e) / math.sqrt(HS)
+    queries[...] = (nn(qf[...], w_q[...]) * scale).astype(BF)
+
     loads[9].wait()
     for c in range(2):
         for k in range(1, shards):
@@ -251,8 +247,6 @@
     attend(kv_own, 0)
     swap.wait()
     attend(kv_far, D)
-    loads[10].wait()
-    out_ref[...] = nn(joined[...], w_out[...]).astype(BF)
 
     for k in range(1, shards):
         q_copy(k, me).wait_send()
@@ -282,10 +276,10 @@
     anchors = anchor_index.shape[1]
     vmem = pl.BlockSpec(memory_space=pltpu.VMEM)
     hbm = pl.BlockSpec(memory_space=pltpu.HBM)
-    result = pl.pallas_call(
+    both = pl.pallas_call(
         functools.partial(kernel, shards),
-        out_shape=jax.ShapeDtypeStruct((rows, D), BF),
-        in_specs=[hbm] * 11,
+        out_shape=jax.ShapeDtypeStruct((rows, 2 * D), BF),
+        in_specs=[hbm] * 10,
         out_specs=vmem,
         scratch_shapes=[
             pltpu.VMEM(supernode_query.shape[1:], BF),
@@ -298,7 +292,6 @@
             pltpu.VMEM((D, D), BF),
             pltpu.VMEM((D, D), BF),
             pltpu.VMEM((D, 2 * D), BF),
-            pltpu.VMEM((2 * D, D), BF),
             pltpu.VMEM((points.shape[0], D), BF),
             pltpu.VMEM((rows, D), BF),
             pltpu.VMEM((nodes, D), BF),
@@ -308,8 +301,7 @@
             pltpu.VMEM((half * HP, D), BF),
             pltpu.VMEM((anchors, 2 * D), BF),
             pltpu.VMEM((anchors, 2 * D), BF),
-            pltpu.VMEM((rows, 2 * D), BF),
-            pltpu.SemaphoreType.DMA((11,)),
+            pltpu.SemaphoreType.DMA((10,)),
             pltpu.SemaphoreType.DMA((shards,)),
             pltpu.SemaphoreType.DMA((shards,)),
             pltpu.SemaphoreType.DMA((2, shards)),
@@ -331,9 +323,8 @@
         w_q[0],
         w_mid[0],
         w_kv[0],
-        w_out[0],
     )
-    return result[None]
+    return nn(both, w_out[0]).astype(BF)[None]
 
 
 def solution(mesh):

time: 36.9 us -> 36.9 us (level)
  matrix products: 0 us -> 3.67 us
  local copies, waits for them, and re-layouts: 2.06 us -> 0.01 us
  Pallas kernels: 34.7 us -> 33.1 us
    dot_general x0 -> x1, matrix products: none -> 3.67 us  [nn(): lax.dot_general(a, b, (((1,), (0,)), ((), ())), preferred_element_type=F32)]
    unnamed x1 -> x2, local copies, waits for them, and re-layouts: 2.06 us -> 0.01 us
    pallas_call x1, Pallas kernels: 34.7 us -> 33.1 us  [per_device(): pl.pallas_call(functools.partial(kernel, shards), out_shape=jax.ShapeDtyp...]
where the time goes in v3:
time: 36.9 us; the launch traced here: 36.8 us
  Pallas kernels  33.1 us (90%)
  matrix products  3.67 us (10%)
    pallas_call x1, Pallas kernels, per_device(): pl.pallas_call(functools.partial(kernel, shards), out_shape=jax.ShapeDtyp...  33.1 us
    dot_general x1, matrix products, nn(): lax.dot_general(a, b, (((1,), (0,)), ((), ())), preferred_element_type=F32)  3.67 us

profile of v3, /device:TPU:0, one launch (start us, length us, event | category | flops | bytes accessed | tf_op | source)
XLA Modules:
  0.0 36.8 jit_solution(15756814448845060317)
XLA Ops:
  0.0 0.0 copy-start
  0.0 33.1 %shard_map.109 = bf16[512,1536]{1,0:T(8,128)(2,1)} custom-call(bf16[32,768]{1,0:T(8,128)(2,1)} %bitcast.24, s32[1,256]{1,0:T(1,128)} %bitcast.25, s32[1,256]{1,0:T(1,128)} %slot_hbm.1, s32[1,192]{1,0:T(1,128)} %anchor_hbm.1, bf16[128,768]{1,0:T(8,128)(2,1)} %bitcast.23, bf16[4096,128]{1,0:T(8,128)(2,1)} %bitcast.21, bf16[512,768]{1,0:T(8,128)(2,1)} %bitcast.22, ...), custom_call_target="tpu_custom_call" | custom-call | tf_op jit(solution)/shard_map/pallas_call | solution.py:279
  33.1 0.0 copy-done
  33.1 3.7 %fusion.5 = bf16[1,512,768]{2,1,0:T(8,128)(2,1)} fusion(bf16[512,1536]{1,0:T(8,128)(2,1)} %shard_map.109, bf16[1,1536,768]{2,1,0:T(8,128)(2,1)S(1)} %copy-done), kind=kOutput, calls=%fused_computation.3 | convolution fusion | flops 1208352768 | bytes 4718592 | tf_op jit(solution)/shard_map/dot_general | solution.py:23
Async XLA Ops:
  0.0 33.1 %copy-start = (bf16[1,1536,768]{2,1,0:T(8,128)(2,1)S(1)}, bf16[1,1536,768]{2,1,0:T(8,128)(2,1)}, u32[]{:S(2)}) copy-start(bf16[1,1536,768]{2,1,0:T(8,128)(2,1)} %param.21) | copy-start | bytes 7077892
